TPU v7x, 256 devices: a whole 4x4x8 slice. The times are simulated.
256 devices in a mesh: prow: 16 (over x, z_hi), pcol: 16 (over z_lo, y, core).
Axes of the slice: x: 4, y: 4, z: 8 (z_hi: 4, z_lo: 2; z = z_hi * 2 + z_lo), core: 2. Of those that a mesh axis runs over, the one named last changes fastest.
Arguments:
- separator_inverse: float32 [12288, 12288], P('prow', 'pcol'), may hold values from -6 to 6
- panel: float32 [12288, 2048], P('pcol', 'prow'), may hold values from -0.0546875 to 0.0546875
- block_rows: int32 [16], replicated, may hold values 0 or 1
- pivot_inverse: float32 [2048, 2048], P('prow', 'pcol'), may hold values from -4 to 4
Outputs:
- off_diagonal: float32 [12288, 2048], P('prow', 'pcol')
- child_inverse: float32 [2048, 2048], P('prow', 'pcol')
All inputs are finite; a program needn't handle non-finite values.
Results may differ from a plain program's by a relative error of at most 0.000088.
Values sent between devices are 32-bit elements; how exact they have to be, the bound alone decides.
No kernel may reach another device: no remote copies, remote signals or barrier semaphores. Data moves between devices by JAX's collectives and lax.ppermute only.
A program may use at most 128 MiB of HBM per device.

v0:
```python
import jax
import jax.numpy as jnp
from jax import lax
from jax.sharding import PartitionSpec as P

BS = 768


def from_root(value, axis, source):
    kept = jnp.where(lax.axis_index(axis) == source, value, 0).astype(value.dtype)
    return lax.psum(kept, axis)


def local(separator_inverse, panel, block_rows, pivot_inverse):
    local_rows = separator_inverse.shape[0]
    local_cols = separator_inverse.shape[1]
    row_index = lax.axis_index("prow")
    col_index = lax.axis_index("pcol")
    row_blocks = local_rows // BS
    col_blocks = local_cols // BS
    col_keep = lax.dynamic_slice_in_dim(block_rows, col_index * col_blocks, col_blocks).astype(
        jnp.float32
    )
    masked = (panel.reshape(col_blocks, BS, panel.shape[1]) * col_keep[:, None, None]).reshape(
        panel.shape
    )
    whole_panel = lax.all_gather(masked, "prow", axis=1, tiled=True)
    child_width = whole_panel.shape[1]
    share = child_width // lax.axis_size("pcol")
    part = lax.psum_scatter(
        lax.dot_general(
            whole_panel,
            separator_inverse,
            (((0,), (1,)), ((), ())),
            precision=lax.Precision.HIGHEST,
            preferred_element_type=jnp.float32,
        ),
        "pcol",
        scatter_dimension=0,
        tiled=True,
    )
    root = row_index * lax.axis_size("pcol") // lax.axis_size("prow")
    panel_piece = from_root(whole_panel, "pcol", root)
    row_keep = lax.dynamic_slice_in_dim(block_rows, row_index * row_blocks, row_blocks).astype(
        jnp.float32
    )
    kept = (part.reshape(share, row_blocks, BS) * row_keep[None, :, None]).reshape(
        share, local_rows
    )
    off_diagonal = -kept.T
    gram_part = lax.dot_general(
        panel_piece,
        kept,
        (((0,), (1,)), ((), ())),
        precision=lax.Precision.HIGHEST,
        preferred_element_type=jnp.float32,
    )
    gram_share = lax.psum_scatter(gram_part, "prow", scatter_dimension=0, tiled=True)
    child_inverse = pivot_inverse + gram_share
    return (off_diagonal, child_inverse)


def solution(mesh):
    in_specs = (P("prow", "pcol"), P("pcol", "prow"), P(), P("prow", "pcol"))
    out_specs = (P("prow", "pcol"), P("prow", "pcol"))
    return jax.shard_map(local, mesh=mesh, in_specs=in_specs, out_specs=out_specs, check_vma=False)
```

profile of v0, /device:TPU:24, one launch (start us, length us, event | category | flops | bytes accessed | tf_op | source)
XLA Modules:
  0.0 444.3 jit_solution(6363968940040066956)
XLA Ops:
  7.2 0.0 copy-start
  7.2 0.0 all-gather.2.cloned.1.call-start
  7.2 1.4 fusion.3
  9.3 1.8 broadcast_multiply_fusion
  11.1 0.0 all-gather.2.cloned.1.call-update
  11.1 0.0 all-reduce.2.cloned.1.call-start
  11.2 106.4 %all-gather.2.cloned.1.call-done = f32[768,2048]{1,0:T(8,128)} async-done(((f32[768,128]{1,0:T(8,128)}), f32[768,2048]{1,0:T(8,128)}) %all-gather.2.cloned.1.call-update) | async-done | bytes 6291472 | tf_op jit(solution)/shard_map/all_gather | solution.py:27
  117.6 3.7 broadcast_select_fusion
  121.3 0.0 all-reduce.2.cloned.1.call-update
  121.3 0.0 reduce-scatter.3.cloned.1.call-start
  121.4 0.0 copy-done
  121.4 33.1 %fusion.4 = f32[2048,768]{1,0:T(8,128)} fusion(f32[768,2048]{1,0:T(8,128)} %all-gather.2.cloned.1.call-done, f32[768,768]{1,0:T(8,128)S(1)} %copy-done), kind=kOutput, calls=%fused_computation.7 | convolution fusion | flops 14495514624 | bytes 14942208 | tf_op jit(solution)/shard_map/dot_general | solution.py:31
  154.5 0.0 reduce-scatter.3.cloned.1.call-update
  154.5 0.0 copy-start.2
  154.5 0.0 reduce-scatter.5.cloned.1.call-start
  155.2 102.8 %all-reduce.2.cloned.1.call-done = f32[768,2048]{1,0:T(8,128)} async-done(((f32[768,2048]{1,0:T(8,128)}), f32[768,2048]{1,0:T(8,128)}) %all-reduce.2.cloned.1.call-update) | async-done | bytes 6291472 | tf_op jit(solution)/shard_map/psum | solution.py:11
  258.1 75.7 %reduce-scatter.3.cloned.1.call-done = f32[128,768]{1,0:T(8,128)} async-done(((f32[2048,768]{1,0:T(8,128)}), f32[128,768]{1,0:T(8,128)}) %reduce-scatter.3.cloned.1.call-update) | async-done | bytes 393232 | tf_op jit(solution)/shard_map/reduce_scatter | solution.py:30
  333.7 0.0 copy-start.1
  333.8 13.6 %fusion = f32[2048,128]{1,0:T(8,128)} fusion(f32[768,2048]{1,0:T(8,128)} %all-reduce.2.cloned.1.call-done, f32[128,768]{1,0:T(8,128)} %reduce-scatter.3.cloned.1.call-done, f32[]{:T(128)} %bitcast.1), kind=kOutput, calls=%fused_computation.2 | convolution fusion | flops 2416017408 | bytes 7733252 | tf_op jit(solution)/shard_map/dot_general | solution.py:51
  347.3 0.0 reduce-scatter.5.cloned.1.call-update
  347.4 0.0 copy-done.1
  347.4 0.9 copy.6
  348.3 87.9 %reduce-scatter.5.cloned.1.call-done = f32[128,128]{1,0:T(8,128)} async-done(((f32[2048,128]{1,0:T(8,128)}), f32[128,128]{1,0:T(8,128)}) %reduce-scatter.5.cloned.1.call-update) | async-done | bytes 65552 | tf_op jit(solution)/shard_map/reduce_scatter | solution.py:58
  436.3 0.0 copy-done.2
  436.3 1.5 add.18
  (1 shorter events, 0.0 us)
Async XLA Ops:
  7.2 114.2 %copy-start = (f32[768,768]{1,0:T(8,128)S(1)}, f32[768,768]{1,0:T(8,128)}, u32[]{:S(2)}) copy-start(f32[768,768]{1,0:T(8,128)} %param.4) | copy-start | bytes 7077892
  7.2 110.4 %all-gather.2.cloned.1.call-start = ((), (), s32[]{:S(2)}) async-start(), calls=%async_computation.2 | async-start | bytes 6684672 | tf_op jit(solution)/shard_map/all_gather | solution.py:27
  11.1 247.0 %all-reduce.2.cloned.1.call-start = ((), (), s32[]{:S(2)}) async-start(), calls=%async_computation.4 | async-start | bytes 12582912 | tf_op jit(solution)/shard_map/psum | solution.py:11
  121.3 212.4 %reduce-scatter.3.cloned.1.call-start = ((), (), s32[]{:S(2)}) async-start(), calls=%async_computation.3 | async-start | bytes 6684672 | tf_op jit(solution)/shard_map/reduce_scatter | solution.py:30
  154.5 281.7 %copy-start.2 = (f32[128,128]{1,0:T(8,128)S(1)}, f32[128,128]{1,0:T(8,128)}, u32[]{:S(2)}) copy-start(f32[128,128]{1,0:T(8,128)} %param.7) | copy-start | bytes 196612
  154.5 281.7 %reduce-scatter.5.cloned.1.call-start = ((), (), s32[]{:S(2)}) async-start(), calls=%async_computation.5 | async-start | bytes 1114112 | tf_op jit(solution)/shard_map/reduce_scatter | solution.py:58
  333.7 13.6 %copy-start.1 = (f32[128,768]{1,0:T(8,128)S(1)}, f32[128,768]{1,0:T(8,128)}, u32[]{:S(2)}) copy-start(f32[128,768]{1,0:T(8,128)} %reduce-scatter.3.cloned.1.call-done) | copy-start | bytes 1179652
Sparse Core Ops, SparseCore 0:
  11.2 106.3 all-gather.1
  121.5 136.5 all-reduce.1
  260.6 73.0 reduce-scatter.2
  347.5 88.7 reduce-scatter.4
where the time goes:
time: 445 us; the launch traced here: 444 us
  waiting for transfers between devices  373 us (84%)
  matrix products  46.7 us (10%)
  between operations  15.1 us (3%)
  other arithmetic  7 us (2%)
    all_gather x1, waiting for transfers between devices, local(): whole_panel = lax.all_gather(masked, 'prow', axis=1, tiled=True)  106 us
    psum x1, waiting for transfers between devices, from_root(): return lax.psum(kept, axis)  103 us
    reduce_scatter x1, waiting for transfers between devices, local(): lax.psum_scatter(gram_part, 'prow', scatter_dimension=0, tiled=True)  87.9 us
    reduce_scatter x1, waiting for transfers between devices, local(): lax.psum_scatter(lax.dot_general(whole_panel, separator_inverse, (((0,),...  75.7 us
    dot_general x1, matrix products, local(): lax.dot_general(whole_panel, separator_inverse, (((0,), (1,)), ((), ())),...  33.1 us
    dot_general x1, matrix products, local(): lax.dot_general(panel_piece, kept, (((0,), (1,)), ((), ())), precision=la...  13.6 us
  transfers between devices with their start and end apart: 4, of which 4 were waited for; matrix products, arithmetic and copies ran while one was open for 8% of the time, Pallas kernels for 0%

commit v1 on v0

v1 whole, which is shorter than its diff:
```python
import jax
import jax.numpy as jnp
from jax import lax
from jax.sharding import PartitionSpec as P

BS = 768
AXES = ("prow", "pcol")
CHUNKS = 1


def places():
    for x in range(4):
        for zh in range(4):
            for zl in range(2):
                for y in range(4):
                    for core in range(2):
                        yield x, zh, zl, y, core


def index_of(x, zh, zl, y, core):
    return ((x % 4) * 4 + zh % 4) * 16 + (zl % 2) * 8 + (y % 4) * 2 + core % 2


def shift(dx=0, dzh=0, dzl=0, dy=0, dcore=0):
    return [
        (index_of(x, zh, zl, y, c), index_of(x + dx, zh + dzh, zl + dzl, y + dy, c + dcore))
        for x, zh, zl, y, c in places()
    ]


def spot(r, i):
    x, zh = i >> 2, i & 3
    return ((zh & 1) ^ (r >> 3)) * 8 + ((x + zh) % 4) * 2 + (zh >> 1)


def block_at(r, c):
    zl, y, core = c >> 3, (c >> 1) & 3, c & 1
    zh = (zl ^ (r >> 3)) + 2 * core
    return lax.rem(y - zh + 4, 4) * 4 + zh


TO_ROW = [(i * 16 + r, r * 16 + spot(r, i)) for i in range(16) for r in range(16)]


def send(value, pairs):
    return lax.ppermute(value, AXES, pairs)


def ring_gather(value, me, axis):
    out = jnp.zeros((4,) + value.shape, value.dtype)
    out = lax.dynamic_update_index_in_dim(out, value, me, 0)
    for step in (1, -1, 2):
        got = send(value, shift(**{axis: step}))
        out = lax.dynamic_update_index_in_dim(out, got, lax.rem(me - step + 4, 4), 0)
    return out


def ring_scatter(value, me, axis, dim):
    pick = lambda place: lax.dynamic_index_in_dim(value, lax.rem(place + 4, 4), dim, keepdims=False)
    got = [send(pick(me + step), shift(**{axis: step})) for step in (1, -1, 2)]
    return (pick(me) + got[0]) + (got[1] + got[2])


def dot_t(a, b):
    return lax.dot_general(
        a, b, (((1,), (1,)), ((), ())), precision=lax.Precision.HIGH, preferred_element_type=jnp.float32
    )


def local(separator_inverse, panel, block_rows, pivot_inverse):
    r = lax.axis_index("prow")
    c = lax.axis_index("pcol")
    x, zh = r // 4, lax.rem(r, 4)
    zl, y, core = c // 8, lax.rem(c // 2, 4), lax.rem(c, 2)
    first = core == 0
    keep_c = lax.dynamic_index_in_dim(block_rows, c, 0, keepdims=False).astype(jnp.float32)
    keep_r = lax.dynamic_index_in_dim(block_rows, r, 0, keepdims=False).astype(jnp.float32)
    swap = shift(dcore=1)

    panel_t = (panel * keep_c).T
    low, high = panel_t[:64], panel_t[64:]
    mine = jnp.where(first, low, high)
    theirs = jnp.where(first, high, low)
    mine = jnp.concatenate([mine, send(theirs, swap)], axis=1)
    sep = jnp.concatenate([separator_inverse, send(separator_inverse, swap)], axis=1)

    rows = 64 // CHUNKS
    halves = []
    for t in range(CHUNKS):
        part = mine[rows * t : rows * (t + 1)]
        part = ring_gather(part, zh, "dzh")
        part = ring_gather(part, x, "dx")
        sums = dot_t(part.reshape(16 * rows, 2 * BS), sep)
        sums = ring_scatter(sums.reshape(2, 4, 2, rows, BS), y, "dy", 1)
        other = lax.dynamic_index_in_dim(sums, 1 - zl, 0, keepdims=False)
        own = lax.dynamic_index_in_dim(sums, zl, 0, keepdims=False)
        sums = own + send(other, shift(dzl=1))
        halves.append(sums)

    sums = halves[0] if CHUNKS == 1 else jnp.concatenate(halves, axis=1)
    other = lax.dynamic_index_in_dim(sums, 1 - core, 0, keepdims=False)
    own = lax.dynamic_index_in_dim(sums, core, 0, keepdims=False)
    got = send(other, swap)
    kept = keep_r * jnp.where(first, jnp.concatenate([own, got]), jnp.concatenate([got, own]))
    off_diagonal = -kept.T

    piece = send(panel_t, TO_ROW)
    pieces = jnp.stack([piece, send(piece, shift(dzl=1))])
    pieces = jnp.stack([pieces] + [send(pieces, shift(dy=s)) for s in (1, -1, 2)])
    pieces = jnp.stack([pieces, send(pieces, swap)])
    row_panel = jnp.zeros((16, 128, BS), jnp.float32)
    for dc in range(2):
        for dy, step in enumerate((0, 1, -1, 2)):
            for dz in range(2):
                place = (zl ^ dz) * 8 + lax.rem(y - step + 4, 4) * 2 + (core ^ dc)
                row_panel = lax.dynamic_update_index_in_dim(row_panel, pieces[dc, dy, dz], block_at(r, place), 0)

    gram = dot_t(row_panel.reshape(2048, BS), kept).reshape(4, 4, 128, 128)
    gram = ring_scatter(gram, x, "dx", 0)
    gram = ring_scatter(gram, zh, "dzh", 0)
    return off_diagonal, pivot_inverse + gram


def solution(mesh):
    in_specs = (P("prow", "pcol"), P("pcol", "prow"), P(), P("prow", "pcol"))
    out_specs = (P("prow", "pcol"), P("prow", "pcol"))
    return jax.shard_map(local, mesh=mesh, in_specs=in_specs, out_specs=out_specs, check_vma=False)
```

time: 445 us -> 254 us (0.57)
  waiting for transfers between devices: 373 us -> 160 us
  starting transfers between devices: 0.16 us -> 64.8 us
  matrix products: 46.7 us -> 13.4 us
  between operations: 15.1 us -> 2.48 us
  local copies, waits for them, and re-layouts: 2.35 us -> 7.79 us
    reduce_scatter x2 -> x0, waiting for transfers between devices: 164 us -> none  [the longest x1 87.9 us: local(): lax.psum_scatter(gram_part, 'prow', scatter_dimension=0, tiled=True)]
    ppermute x0 -> x25, waiting for transfers between devices: none -> 160 us  [send(): return lax.ppermute(value, AXES, pairs)]
    all_gather x1 -> x0, waiting for transfers between devices: 106 us -> none  [local(): whole_panel = lax.all_gather(masked, 'prow', axis=1, tiled=True)]
    psum x1 -> x0, waiting for transfers between devices: 103 us -> none  [from_root(): return lax.psum(kept, axis)]
    ppermute x0 -> x25, starting transfers between devices: none -> 64.8 us  [send(): return lax.ppermute(value, AXES, pairs)]
    dot_general x2, matrix products: 46.7 us -> 13.4 us  [dot_t(): lax.dot_general(a, b, (((1,), (1,)), ((), ())), precision=lax.Precision.H...]
  transfers between devices with their start and end apart: 4 -> 25, of which waited for: 4 -> 17; matrix products, arithmetic and copies ran while one was open for 8% -> 8% of each run, Pallas kernels for 0% -> 0%
where the time goes in v1:
time: 254 us; the launch traced here: 252 us
  waiting for transfers between devices  160 us (63%)
  starting transfers between devices  64.8 us (26%)
  matrix products  13.4 us (5%)
  local copies, waits for them, and re-layouts  7.79 us (3%)
  other arithmetic  4.08 us (2%)
    ppermute x25, waiting for transfers between devices, send(): return lax.ppermute(value, AXES, pairs)  160 us
    ppermute x25, starting transfers between devices, send(): return lax.ppermute(value, AXES, pairs)  64.8 us
    dot_general x2, matrix products, dot_t(): lax.dot_general(a, b, (((1,), (1,)), ((), ())), precision=lax.Precision.H...  13.4 us
  transfers between devices with their start and end apart: 25, of which 17 were waited for; matrix products, arithmetic and copies ran while one was open for 8% of the time, Pallas kernels for 0%

profile of v1, /device:TPU:24, one launch (start us, length us, event | category | flops | bytes accessed | tf_op | source)
XLA Modules:
  0.0 252.3 jit_solution(2527753070604048920)
XLA Ops:
  4.0 9.7 %collective-permute-start.13 = (f32[128,768]{1,0:T(8,128)S(1)}, f32[128,768]{1,0:T(8,128)S(1)}, u32[]{:S(2)}, u32[]{:S(2)}) collective-permute-start(f32[128,768]{1,0:T(8,128)S(1)} %multiply_bitcast_fusion), channel_id=1, source_target_pairs={{0,0},{1,16},{2,32},{3,48},{4,64},{5,80},{6,96},{7,112},{8,136},{9... | collective-permute-start | bytes 1179656 | tf_op jit(solution)/shard_map/ppermute | solution.py:46
  13.7 2.1 collective-permute-start.1
  15.8 2.1 collective-permute-start.2
  17.9 1.6 collective-permute-start.3
  19.7 9.3 %collective-permute-done.13 = f32[128,768]{1,0:T(8,128)S(1)} collective-permute-done((f32[128,768]{1,0:T(8,128)S(1)}, f32[128,768]{1,0:T(8,128)S(1)}, u32[]{:S(2)}, u32[]{:S(2)}) %collective-permute-start.13) | collective-permute-done | bytes 393248 | tf_op jit(solution)/shard_map/ppermute | solution.py:46
  29.0 8.2 %collective-permute-start.14 = (f32[128,768]{1,0:T(8,128)S(1)}, f32[128,768]{1,0:T(8,128)S(1)}, u32[]{:S(2)}, u32[]{:S(2)}) collective-permute-start(f32[128,768]{1,0:T(8,128)S(1)} %collective-permute-done.13), channel_id=1, source_target_pairs={{0,8},{1,9},{2,10},{3,11},{4,12},{5,13},{6,14},{7,15},{8,0},{9,1},... | collective-permute-start | bytes 1179656 | tf_op jit(solution)/shard_map/ppermute | solution.py:46
  37.2 2.7 %collective-permute-done.1 = f32[64,1536]{1,0:T(8,128)S(1)} collective-permute-done((f32[64,1536]{1,0:T(8,128)S(1)}, f32[64,1536]{1,0:T(8,128)S(1)}, u32[]{:S(2)}, u32[]{:S(2)}) %collective-permute-start.1) | collective-permute-done | bytes 393248 | tf_op jit(solution)/shard_map/ppermute | solution.py:46
  39.9 14.7 %collective-permute-done.2 = f32[64,1536]{1,0:T(8,128)S(1)} collective-permute-done((f32[64,1536]{1,0:T(8,128)S(1)}, f32[64,1536]{1,0:T(8,128)S(1)}, u32[]{:S(2)}, u32[]{:S(2)}) %collective-permute-start.2) | collective-permute-done | bytes 393248 | tf_op jit(solution)/shard_map/ppermute | solution.py:46
  54.6 16.9 %collective-permute-done.14 = f32[128,768]{1,0:T(8,128)S(1)} collective-permute-done((f32[128,768]{1,0:T(8,128)S(1)}, f32[128,768]{1,0:T(8,128)S(1)}, u32[]{:S(2)}, u32[]{:S(2)}) %collective-permute-start.14) | collective-permute-done | bytes 393248 | tf_op jit(solution)/shard_map/ppermute | solution.py:46
  72.6 1.9 collective-permute-start.4
  74.5 3.2 %collective-permute-start.15 = (f32[2,128,768]{2,1,0:T(8,128)}, f32[2,128,768]{2,1,0:T(8,128)}, u32[]{:S(2)}, u32[]{:S(2)}) collective-permute-start(f32[2,128,768]{2,1,0:T(8,128)} %get-tuple-element.13), channel_id=1, source_target_pairs={{0,2},{1,3},{2,4},{3,5},{4,6},{5,7},{6,0},{7,1},{8,10},{9,11},{10,... | collective-permute-start | bytes 2359304 | tf_op jit(solution)/shard_map/ppermute | solution.py:46
  78.5 16.3 %collective-permute-done.17 = f32[2,128,768]{2,1,0:T(8,128)S(1)} collective-permute-done((f32[2,128,768]{2,1,0:T(8,128)}, f32[2,128,768]{2,1,0:T(8,128)S(1)}, u32[]{:S(2)}, u32[]{:S(2)}) %collective-permute-start.17) | collective-permute-done | bytes 786464 | tf_op jit(solution)/shard_map/ppermute | solution.py:46
  95.8 14.2 %collective-permute-done.16 = f32[2,128,768]{2,1,0:T(8,128)} collective-permute-done((f32[2,128,768]{2,1,0:T(8,128)}, f32[2,128,768]{2,1,0:T(8,128)}, u32[]{:S(2)}, u32[]{:S(2)}) %collective-permute-start.16) | collective-permute-done | bytes 786464 | tf_op jit(solution)/shard_map/ppermute | solution.py:46
  110.0 3.1 %collective-permute-start.6 = (f32[4,64,1536]{2,1,0:T(8,128)S(1)}, f32[4,64,1536]{2,1,0:T(8,128)S(1)}, u32[]{:S(2)}, u32[]{:S(2)}) collective-permute-start(f32[4,64,1536]{2,1,0:T(8,128)S(1)} %bitcast_dynamic-update-slice_fusion.4), channel_id=1, source_target_pairs={{0,128},{1,129},{2,130},{3,131},{4,132},{5,133},{6,134},{7,135},{8... | collective-permute-start | bytes 4718600 | tf_op jit(solution)/shard_map/ppermute | solution.py:46
  113.1 2.0 pad_maximum_fusion
  117.6 43.7 %collective-permute-done.5 = f32[4,64,1536]{2,1,0:T(8,128)S(1)} collective-permute-done((f32[4,64,1536]{2,1,0:T(8,128)S(1)}, f32[4,64,1536]{2,1,0:T(8,128)S(1)}, u32[]{:S(2)}, u32[]{:S(2)}) %collective-permute-start.5) | collective-permute-done | bytes 1572896 | tf_op jit(solution)/shard_map/ppermute | solution.py:46
  161.6 10.7 %fusion = f32[2,4,2,64,768]{4,3,2,1,0:T(8,128)S(1)} fusion(f32[2,4,2,64,1536]{4,3,2,1,0:T(8,128)S(1)} %bitcast.151, f32[768,768]{1,0:T(8,128)} %collective-permute-done.7, f32[768,768]{1,0:T(8,128)} %param.4), kind=kOutput, calls=%fused_computation.1 | convolution fusion | flops 7248936960 | bytes 14155776 | tf_op jit(solution)/shard_map/dot_general | solution.py:65
  172.6 2.0 collective-permute-start.9
  174.6 2.9 %collective-permute-start.10 = (f32[2,2,64,768]{3,2,1,0:T(8,128)S(1)}, f32[2,2,64,768]{3,2,1,0:T(8,128)S(1)}, u32[]{:S(2)}, u32[]{:S(2)}) collective-permute-start(f32[2,2,64,768]{3,2,1,0:T(8,128)S(1)} %get-tuple-element.6), channel_id=1, source_target_pairs={{0,4},{1,5},{2,6},{3,7},{4,0},{5,1},{6,2},{7,3},{8,12},{9,13},{10,... | collective-permute-start | bytes 2359304 | tf_op jit(solution)/shard_map/ppermute | solution.py:46
  177.7 8.4 %collective-permute-done.8 = f32[2,2,64,768]{3,2,1,0:T(8,128)S(1)} collective-permute-done((f32[2,2,64,768]{3,2,1,0:T(8,128)S(1)}, f32[2,2,64,768]{3,2,1,0:T(8,128)S(1)}, u32[]{:S(2)}, u32[]{:S(2)}) %collective-permute-start.8) | collective-permute-done | bytes 786464 | tf_op jit(solution)/shard_map/ppermute | solution.py:46
  187.3 8.6 %collective-permute-done.10 = f32[2,2,64,768]{3,2,1,0:T(8,128)S(1)} collective-permute-done((f32[2,2,64,768]{3,2,1,0:T(8,128)S(1)}, f32[2,2,64,768]{3,2,1,0:T(8,128)S(1)}, u32[]{:S(2)}, u32[]{:S(2)}) %collective-permute-start.10) | collective-permute-done | bytes 786464 | tf_op jit(solution)/shard_map/ppermute | solution.py:46
  196.1 12.2 %collective-permute-start.11 = (f32[2,64,768]{2,1,0:T(8,128)S(1)}, f32[2,64,768]{2,1,0:T(8,128)S(1)}, u32[]{:S(2)}, u32[]{:S(2)}) collective-permute-start(f32[2,64,768]{2,1,0:T(8,128)S(1)} %dynamic-slice_bitcast_fusion.3), channel_id=1, source_target_pairs={{0,8},{1,9},{2,10},{3,11},{4,12},{5,13},{6,14},{7,15},{8,0},{9,1},... | collective-permute-start | bytes 1179656 | tf_op jit(solution)/shard_map/ppermute | solution.py:46
  208.4 5.7 %collective-permute-done.11 = f32[2,64,768]{2,1,0:T(8,128)S(1)} collective-permute-done((f32[2,64,768]{2,1,0:T(8,128)S(1)}, f32[2,64,768]{2,1,0:T(8,128)S(1)}, u32[]{:S(2)}, u32[]{:S(2)}) %collective-permute-start.11) | collective-permute-done | bytes 393248 | tf_op jit(solution)/shard_map/ppermute | solution.py:46
  215.7 2.6 %fusion.21 = f32[4,4,128,128]{3,2,1,0:T(8,128)S(1)} fusion(f32[4,4,128,768]{3,2,1,0:T(8,128)S(1)} %bitcast.150, f32[64,768]{1,0:T(8,128)S(1)} %collective-permute-done.12, f32[64,768]{1,0:T(8,128)S(1)} %get-tuple-element.15, f32[]{:T(128)} %bitcast, pred[]{:T(512)S(6)} %eq.3), kind=kOutput, calls=%fused_computation.50 | convolution fusion | flops 1208352768 | bytes 7733253 | tf_op jit(solution)/shard_map/dot_general | solution.py:65
  218.4 2.3 collective-permute-start.19
  220.7 4.6 %collective-permute-start.20 = (f32[4,128,128]{2,1,0:T(8,128)S(1)}, f32[4,128,128]{2,1,0:T(8,128)S(1)}, u32[]{:S(2)}, u32[]{:S(2)}) collective-permute-start(f32[4,128,128]{2,1,0:T(8,128)S(1)} %get-tuple-element.10), channel_id=1, source_target_pairs={{0,192},{1,193},{2,194},{3,195},{4,196},{5,197},{6,198},{7,199},{8... | collective-permute-start | bytes 786440 | tf_op jit(solution)/shard_map/ppermute | solution.py:46
  226.5 5.1 %collective-permute-done.19 = f32[4,128,128]{2,1,0:T(8,128)S(1)} collective-permute-done((f32[4,128,128]{2,1,0:T(8,128)S(1)}, f32[4,128,128]{2,1,0:T(8,128)S(1)}, u32[]{:S(2)}, u32[]{:S(2)}) %collective-permute-start.19) | collective-permute-done | bytes 262176 | tf_op jit(solution)/shard_map/ppermute | solution.py:46
  231.6 5.2 %collective-permute-done.20 = f32[4,128,128]{2,1,0:T(8,128)S(1)} collective-permute-done((f32[4,128,128]{2,1,0:T(8,128)S(1)}, f32[4,128,128]{2,1,0:T(8,128)S(1)}, u32[]{:S(2)}, u32[]{:S(2)}) %collective-permute-start.20) | collective-permute-done | bytes 262176 | tf_op jit(solution)/shard_map/ppermute | solution.py:46
  236.8 1.6 collective-permute-done.21
  238.5 3.6 %collective-permute-start.22 = (f32[128,128]{1,0:T(8,128)S(1)}, f32[128,128]{1,0:T(8,128)S(1)}, u32[]{:S(2)}, u32[]{:S(2)}) collective-permute-start(f32[128,128]{1,0:T(8,128)S(1)} %get-tuple-element.20), channel_id=1, source_target_pairs={{0,16},{1,17},{2,18},{3,19},{4,20},{5,21},{6,22},{7,23},{8,24},{9,... | collective-permute-start | bytes 196616 | tf_op jit(solution)/shard_map/ppermute | solution.py:46
  243.2 2.5 collective-permute-start.24
  247.8 3.9 %collective-permute-done.24 = f32[128,128]{1,0:T(8,128)S(1)} collective-permute-done((f32[128,128]{1,0:T(8,128)S(1)}, f32[128,128]{1,0:T(8,128)S(1)}, u32[]{:S(2)}, u32[]{:S(2)}) %collective-permute-start.24) | collective-permute-done | bytes 65568 | tf_op jit(solution)/shard_map/ppermute | solution.py:46
  (67 shorter events, 16.3 us)
Async XLA Ops:
  3.9 9.8 %collective-permute-start = (f32[64,768]{1,0:T(8,128)S(1)}, f32[64,768]{1,0:T(8,128)S(1)}, u32[]{:S(2)}, u32[]{:S(2)}) collective-permute-start(f32[64,768]{1,0:T(8,128)S(1)} %get-tuple-element.17), channel_id=1, source_target_pairs={{0,1},{1,0},{2,3},{3,2},{4,5},{5,4},{6,7},{7,6},{8,9},{9,8},{10,11... | collective-permute-start | bytes 589832 | tf_op jit(solution)/shard_map/ppermute | solution.py:46
  4.0 25.0 %collective-permute-start.13 = (f32[128,768]{1,0:T(8,128)S(1)}, f32[128,768]{1,0:T(8,128)S(1)}, u32[]{:S(2)}, u32[]{:S(2)}) collective-permute-start(f32[128,768]{1,0:T(8,128)S(1)} %multiply_bitcast_fusion), channel_id=1, source_target_pairs={{0,0},{1,16},{2,32},{3,48},{4,64},{5,80},{6,96},{7,112},{8,136},{9... | collective-permute-start | bytes 1179656 | tf_op jit(solution)/shard_map/ppermute | solution.py:46
  13.7 26.2 %collective-permute-start.1 = (f32[64,1536]{1,0:T(8,128)S(1)}, f32[64,1536]{1,0:T(8,128)S(1)}, u32[]{:S(2)}, u32[]{:S(2)}) collective-permute-start(f32[64,1536]{1,0:T(8,128)S(1)} %pad_maximum_fusion.2), channel_id=1, source_target_pairs={{0,16},{1,17},{2,18},{3,19},{4,20},{5,21},{6,22},{7,23},{8,24},{9,... | collective-permute-start | bytes 1179656 | tf_op jit(solution)/shard_map/ppermute | solution.py:46
  15.8 38.8 %collective-permute-start.2 = (f32[64,1536]{1,0:T(8,128)S(1)}, f32[64,1536]{1,0:T(8,128)S(1)}, u32[]{:S(2)}, u32[]{:S(2)}) collective-permute-start(f32[64,1536]{1,0:T(8,128)S(1)} %pad_maximum_fusion.2), channel_id=1, source_target_pairs={{0,48},{1,49},{2,50},{3,51},{4,52},{5,53},{6,54},{7,55},{8,56},{9,... | collective-permute-start | bytes 1179656 | tf_op jit(solution)/shard_map/ppermute | solution.py:46
  17.9 54.7 %collective-permute-start.3 = (f32[64,1536]{1,0:T(8,128)S(1)}, f32[64,1536]{1,0:T(8,128)S(1)}, u32[]{:S(2)}, u32[]{:S(2)}) collective-permute-start(f32[64,1536]{1,0:T(8,128)S(1)} %pad_maximum_fusion.2), channel_id=1, source_target_pairs={{0,32},{1,33},{2,34},{3,35},{4,36},{5,37},{6,38},{7,39},{8,40},{9,... | collective-permute-start | bytes 1179656 | tf_op jit(solution)/shard_map/ppermute | solution.py:46
  29.0 42.6 %collective-permute-start.14 = (f32[128,768]{1,0:T(8,128)S(1)}, f32[128,768]{1,0:T(8,128)S(1)}, u32[]{:S(2)}, u32[]{:S(2)}) collective-permute-start(f32[128,768]{1,0:T(8,128)S(1)} %collective-permute-done.13), channel_id=1, source_target_pairs={{0,8},{1,9},{2,10},{3,11},{4,12},{5,13},{6,14},{7,15},{8,0},{9,1},... | collective-permute-start | bytes 1179656 | tf_op jit(solution)/shard_map/ppermute | solution.py:46
  72.6 22.2 %collective-permute-start.17 = (f32[2,128,768]{2,1,0:T(8,128)}, f32[2,128,768]{2,1,0:T(8,128)S(1)}, u32[]{:S(2)}, u32[]{:S(2)}) collective-permute-start(f32[2,128,768]{2,1,0:T(8,128)} %get-tuple-element.13), channel_id=1, source_target_pairs={{0,4},{1,5},{2,6},{3,7},{4,0},{5,1},{6,2},{7,3},{8,12},{9,13},{10,... | collective-permute-start | bytes 2359304 | tf_op jit(solution)/shard_map/ppermute | solution.py:46
  72.6 43.4 %collective-permute-start.4 = (f32[4,64,1536]{2,1,0:T(8,128)S(1)}, f32[4,64,1536]{2,1,0:T(8,128)}, u32[]{:S(2)}, u32[]{:S(2)}) collective-permute-start(f32[4,64,1536]{2,1,0:T(8,128)S(1)} %bitcast_dynamic-update-slice_fusion.4), channel_id=1, source_target_pairs={{0,64},{1,65},{2,66},{3,67},{4,68},{5,69},{6,70},{7,71},{8,72},{9,... | collective-permute-start | bytes 4718600 | tf_op jit(solution)/shard_map/ppermute | solution.py:46
  74.5 35.5 %collective-permute-start.16 = (f32[2,128,768]{2,1,0:T(8,128)}, f32[2,128,768]{2,1,0:T(8,128)}, u32[]{:S(2)}, u32[]{:S(2)}) collective-permute-start(f32[2,128,768]{2,1,0:T(8,128)} %get-tuple-element.13), channel_id=1, source_target_pairs={{0,6},{1,7},{2,0},{3,1},{4,2},{5,3},{6,4},{7,5},{8,14},{9,15},{10,... | collective-permute-start | bytes 2359304 | tf_op jit(solution)/shard_map/ppermute | solution.py:46
  74.5 38.6 %collective-permute-start.15 = (f32[2,128,768]{2,1,0:T(8,128)}, f32[2,128,768]{2,1,0:T(8,128)}, u32[]{:S(2)}, u32[]{:S(2)}) collective-permute-start(f32[2,128,768]{2,1,0:T(8,128)} %get-tuple-element.13), channel_id=1, source_target_pairs={{0,2},{1,3},{2,4},{3,5},{4,6},{5,7},{6,0},{7,1},{8,10},{9,11},{10,... | collective-permute-start | bytes 2359304 | tf_op jit(solution)/shard_map/ppermute | solution.py:46
  77.8 83.8 %collective-permute-start.7 = (f32[768,768]{1,0:T(8,128)}, f32[768,768]{1,0:T(8,128)}, u32[]{:S(2)}, u32[]{:S(2)}) collective-permute-start(f32[768,768]{1,0:T(8,128)} %param.4), channel_id=1, source_target_pairs={{0,1},{1,0},{2,3},{3,2},{4,5},{5,4},{6,7},{7,6},{8,9},{9,8},{10,11... | collective-permute-start | bytes 7077896 | tf_op jit(solution)/shard_map/ppermute | solution.py:46
  94.8 66.5 %collective-permute-start.5 = (f32[4,64,1536]{2,1,0:T(8,128)S(1)}, f32[4,64,1536]{2,1,0:T(8,128)S(1)}, u32[]{:S(2)}, u32[]{:S(2)}) collective-permute-start(f32[4,64,1536]{2,1,0:T(8,128)S(1)} %bitcast_dynamic-update-slice_fusion.4), channel_id=1, source_target_pairs={{0,192},{1,193},{2,194},{3,195},{4,196},{5,197},{6,198},{7,199},{8... | collective-permute-start | bytes 4718600 | tf_op jit(solution)/shard_map/ppermute | solution.py:46
  110.0 51.4 %collective-permute-start.6 = (f32[4,64,1536]{2,1,0:T(8,128)S(1)}, f32[4,64,1536]{2,1,0:T(8,128)S(1)}, u32[]{:S(2)}, u32[]{:S(2)}) collective-permute-start(f32[4,64,1536]{2,1,0:T(8,128)S(1)} %bitcast_dynamic-update-slice_fusion.4), channel_id=1, source_target_pairs={{0,128},{1,129},{2,130},{3,131},{4,132},{5,133},{6,134},{7,135},{8... | collective-permute-start | bytes 4718600 | tf_op jit(solution)/shard_map/ppermute | solution.py:46
  115.1 99.2 %collective-permute-start.18 = (f32[4,2,128,768]{3,2,1,0:T(8,128)S(1)}, f32[4,2,128,768]{3,2,1,0:T(8,128)S(1)}, u32[]{:S(2)}, u32[]{:S(2)}) collective-permute-start(f32[4,2,128,768]{3,2,1,0:T(8,128)S(1)} %get-tuple-element.4), channel_id=1, source_target_pairs={{0,1},{1,0},{2,3},{3,2},{4,5},{5,4},{6,7},{7,6},{8,9},{9,8},{10,11... | collective-permute-start | bytes 9437192 | tf_op jit(solution)/shard_map/ppermute | solution.py:46
  172.5 13.5 %collective-permute-start.8 = (f32[2,2,64,768]{3,2,1,0:T(8,128)S(1)}, f32[2,2,64,768]{3,2,1,0:T(8,128)S(1)}, u32[]{:S(2)}, u32[]{:S(2)}) collective-permute-start(f32[2,2,64,768]{3,2,1,0:T(8,128)S(1)} %get-tuple-element.8), channel_id=1, source_target_pairs={{0,2},{1,3},{2,4},{3,5},{4,6},{5,7},{6,0},{7,1},{8,10},{9,11},{10,... | collective-permute-start | bytes 2359304 | tf_op jit(solution)/shard_map/ppermute | solution.py:46
  172.6 14.7 %collective-permute-start.9 = (f32[2,2,64,768]{3,2,1,0:T(8,128)S(1)}, f32[2,2,64,768]{3,2,1,0:T(8,128)S(1)}, u32[]{:S(2)}, u32[]{:S(2)}) collective-permute-start(f32[2,2,64,768]{3,2,1,0:T(8,128)S(1)} %get-tuple-element.7), channel_id=1, source_target_pairs={{0,6},{1,7},{2,0},{3,1},{4,2},{5,3},{6,4},{7,5},{8,14},{9,15},{10,... | collective-permute-start | bytes 2359304 | tf_op jit(solution)/shard_map/ppermute | solution.py:46
  174.6 21.3 %collective-permute-start.10 = (f32[2,2,64,768]{3,2,1,0:T(8,128)S(1)}, f32[2,2,64,768]{3,2,1,0:T(8,128)S(1)}, u32[]{:S(2)}, u32[]{:S(2)}) collective-permute-start(f32[2,2,64,768]{3,2,1,0:T(8,128)S(1)} %get-tuple-element.6), channel_id=1, source_target_pairs={{0,4},{1,5},{2,6},{3,7},{4,0},{5,1},{6,2},{7,3},{8,12},{9,13},{10,... | collective-permute-start | bytes 2359304 | tf_op jit(solution)/shard_map/ppermute | solution.py:46
  196.1 18.0 %collective-permute-start.11 = (f32[2,64,768]{2,1,0:T(8,128)S(1)}, f32[2,64,768]{2,1,0:T(8,128)S(1)}, u32[]{:S(2)}, u32[]{:S(2)}) collective-permute-start(f32[2,64,768]{2,1,0:T(8,128)S(1)} %dynamic-slice_bitcast_fusion.3), channel_id=1, source_target_pairs={{0,8},{1,9},{2,10},{3,11},{4,12},{5,13},{6,14},{7,15},{8,0},{9,1},... | collective-permute-start | bytes 1179656 | tf_op jit(solution)/shard_map/ppermute | solution.py:46
  214.2 1.5 collective-permute-start.12
  215.7 36.0 %copy-start = (f32[128,128]{1,0:T(8,128)S(1)}, f32[128,128]{1,0:T(8,128)}, u32[]{:S(2)}) copy-start(f32[128,128]{1,0:T(8,128)} %param.7) | copy-start | bytes 196612
  218.4 13.2 %collective-permute-start.19 = (f32[4,128,128]{2,1,0:T(8,128)S(1)}, f32[4,128,128]{2,1,0:T(8,128)S(1)}, u32[]{:S(2)}, u32[]{:S(2)}) collective-permute-start(f32[4,128,128]{2,1,0:T(8,128)S(1)} %get-tuple-element.11), channel_id=1, source_target_pairs={{0,64},{1,65},{2,66},{3,67},{4,68},{5,69},{6,70},{7,71},{8,72},{9,... | collective-permute-start | bytes 786440 | tf_op jit(solution)/shard_map/ppermute | solution.py:46
  220.7 16.1 %collective-permute-start.20 = (f32[4,128,128]{2,1,0:T(8,128)S(1)}, f32[4,128,128]{2,1,0:T(8,128)S(1)}, u32[]{:S(2)}, u32[]{:S(2)}) collective-permute-start(f32[4,128,128]{2,1,0:T(8,128)S(1)} %get-tuple-element.10), channel_id=1, source_target_pairs={{0,192},{1,193},{2,194},{3,195},{4,196},{5,197},{6,198},{7,199},{8... | collective-permute-start | bytes 786440 | tf_op jit(solution)/shard_map/ppermute | solution.py:46
  225.3 13.1 %collective-permute-start.21 = (f32[4,128,128]{2,1,0:T(8,128)S(1)}, f32[4,128,128]{2,1,0:T(8,128)S(1)}, u32[]{:S(2)}, u32[]{:S(2)}) collective-permute-start(f32[4,128,128]{2,1,0:T(8,128)S(1)} %get-tuple-element.9), channel_id=1, source_target_pairs={{0,128},{1,129},{2,130},{3,131},{4,132},{5,133},{6,134},{7,135},{8... | collective-permute-start | bytes 786440 | tf_op jit(solution)/shard_map/ppermute | solution.py:46
  238.5 8.2 %collective-permute-start.22 = (f32[128,128]{1,0:T(8,128)S(1)}, f32[128,128]{1,0:T(8,128)S(1)}, u32[]{:S(2)}, u32[]{:S(2)}) collective-permute-start(f32[128,128]{1,0:T(8,128)S(1)} %get-tuple-element.20), channel_id=1, source_target_pairs={{0,16},{1,17},{2,18},{3,19},{4,20},{5,21},{6,22},{7,23},{8,24},{9,... | collective-permute-start | bytes 196616 | tf_op jit(solution)/shard_map/ppermute | solution.py:46
  242.1 5.7 %collective-permute-start.23 = (f32[128,128]{1,0:T(8,128)S(1)}, f32[128,128]{1,0:T(8,128)S(1)}, u32[]{:S(2)}, u32[]{:S(2)}) collective-permute-start(f32[128,128]{1,0:T(8,128)S(1)} %get-tuple-element.19), channel_id=1, source_target_pairs={{0,48},{1,49},{2,50},{3,51},{4,52},{5,53},{6,54},{7,55},{8,56},{9,... | collective-permute-start | bytes 196616 | tf_op jit(solution)/shard_map/ppermute | solution.py:46
  243.2 8.4 %collective-permute-start.24 = (f32[128,128]{1,0:T(8,128)S(1)}, f32[128,128]{1,0:T(8,128)S(1)}, u32[]{:S(2)}, u32[]{:S(2)}) collective-permute-start(f32[128,128]{1,0:T(8,128)S(1)} %get-tuple-element.18), channel_id=1, source_target_pairs={{0,32},{1,33},{2,34},{3,35},{4,36},{5,37},{6,38},{7,39},{8,40},{9,... | collective-permute-start | bytes 196616 | tf_op jit(solution)/shard_map/ppermute | solution.py:46
